TPU v7x, 256 devices: a whole 4x4x8 slice. The times are simulated.
256 devices in a mesh: band: 16 (over z, x_hi), cuts: 16 (over x_lo, y, core).
Axes of the slice: x: 4 (x_hi: 2, x_lo: 2; x = x_hi * 2 + x_lo), y: 4, z: 8, core: 2. Of those that a mesh axis runs over, the one named last changes fastest.
Arguments:
- var_feat: bfloat16 [1310720, 128], P(('band', 'cuts')), may hold values from -6 to 6
- con_feat: bfloat16 [32768, 128], P(('band', 'cuts')), may hold values from -6 to 6
- slot_column_block: int32 [40960], P(('band', 'cuts')), may hold values from 0 to 39
- slot_constraint_block: int32 [40960], P(('band', 'cuts')), may hold values from 0 to 31
- block_count: int32 [256], P(('band', 'cuts')), may hold values from 40 to 160, as said below
- incidence_coefficients: int32 [40960, 128, 128], P(('band', 'cuts')), may hold values from -3 to 4
- con_first: bfloat16 [256, 256], replicated, may hold values from -0.375 to 0.375
- con_bias: float32 [256], replicated, may hold values from -3 to 3
- con_second: bfloat16 [256, 256], replicated, may hold values from -0.375 to 0.375
- con_third: bfloat16 [256, 128], replicated, may hold values from -0.375 to 0.375
- con_gain: float32 [128], replicated, may hold values from 0.1 to 1.9
- con_shift: float32 [128], replicated, may hold values from -3 to 3
- var_first: bfloat16 [256, 256], replicated, may hold values from -0.375 to 0.375
- var_bias: float32 [256], replicated, may hold values from -3 to 3
- var_second: bfloat16 [256, 256], replicated, may hold values from -0.375 to 0.375
- var_third: bfloat16 [256, 128], replicated, may hold values from -0.375 to 0.375
- var_gain: float32 [128], replicated, may hold values from 0.1 to 1.9
- var_shift: float32 [128], replicated, may hold values from -3 to 3
Outputs:
- con_new: bfloat16 [32768, 128], P(('band', 'cuts'))
- var_new: bfloat16 [1310720, 128], P(('band', 'cuts'))
Inputs may be any that keep to these rules, and one draw needn't show every extreme that they name: Each device's live slots are its first block_count slots; in every draw one eighth of the devices hold 160 live slots and some device holds 40.
All inputs are finite; a program needn't handle non-finite values.
Results may differ from a plain program's by a relative error of at most 0.0075.
Values may be sent and summed in bfloat16 or wider, within the bound.
No kernel may reach another device: no remote copies, remote signals or barrier semaphores. Data moves between devices by JAX's collectives and lax.ppermute only.
A program may use at most 128 MiB of HBM per device.

v0:
```python
import functools
import math

import jax
import jax.numpy as jnp
from jax import lax
from jax.experimental import pallas as pl
from jax.experimental.pallas import tpu as pltpu
from jax.sharding import PartitionSpec as P

EPS = 1e-05
F32 = jnp.float32
BF16 = jnp.bfloat16
GROUP = 16


def place(index):
    return index // 8, (index // 2) % 4, index % 2


def position(x, y, core):
    return x * 8 + y * 2 + core


def layer_norm(values, gain, offset):
    center = values - jnp.mean(values, axis=-1, keepdims=True)
    spread = jnp.mean(center * center, axis=-1, keepdims=True)
    return center * lax.rsqrt(spread + EPS) * gain + offset


def node_update(feats, scaled_agg, w_first, bias, w_second, w_third, gain, offset):
    joined = jnp.concatenate([feats, scaled_agg.astype(BF16)], axis=1)
    hidden = jnp.maximum(jnp.dot(joined, w_first, preferred_element_type=F32) + bias, 0.0).astype(BF16)
    middle = jnp.maximum(jnp.dot(hidden, w_second, preferred_element_type=F32), 0.0).astype(BF16)
    output = jnp.dot(middle, w_third, preferred_element_type=F32)
    return layer_norm(feats.astype(F32) + output, gain, offset).astype(BF16)


def clear(acc):
    def body(block, carry):
        acc[block] = jnp.zeros(acc.shape[1:], acc.dtype)
        return carry

    lax.fori_loop(0, acc.shape[0], body, 0)


def to_constraints_kernel(
    me_ref,
    count_ref,
    col_hbm,
    row_hbm,
    coef_hbm,
    feat_hbm,
    keep_ref,
    give_ref,
    half_ref,
    coef_buf,
    feat_buf,
    acc,
    table,
    col_ref,
    row_ref,
    sem,
    feat_sem,
    index_sem,
):
    count = count_ref[0]
    groups = (count + GROUP - 1) // GROUP

    def coefficients(group):
        rows = pl.ds(group * GROUP, GROUP)
        return pltpu.make_async_copy(coef_hbm.at[rows], coef_buf.at[rows], sem.at[group])

    def start(group, carry):
        coefficients(group).start()
        return carry

    col_copy = pltpu.make_async_copy(col_hbm, col_ref, index_sem.at[0])
    row_copy = pltpu.make_async_copy(row_hbm, row_ref, index_sem.at[1])
    feat_copy = pltpu.make_async_copy(feat_hbm, feat_buf, feat_sem)
    col_copy.start()
    row_copy.start()
    coefficients(0).start()
    feat_copy.start()
    lax.fori_loop(1, groups, start, 0)
    my_x, my_y, my_core = place(me_ref[0] % 16)
    for q in range(32):
        x, y, core = place(q % 16)
        table[q] = (core ^ my_core) * 16 + ((y - my_y) & 3) * 4 + (x ^ my_x) * 2 + q // 16
    clear(acc)
    col_copy.wait()
    row_copy.wait()
    feat_copy.wait()

    def step(group, carry):
        coefficients(group).wait()
        for k in range(GROUP):
            slot = group * GROUP + k
            block = jnp.where(slot < count, table[row_ref[slot]], 32)
            coef = coef_buf[slot].astype(BF16)
            half_ref[slot] = coef
            acc[block] += jnp.dot(coef, feat_buf[col_ref[slot]], preferred_element_type=F32)
        return carry

    lax.fori_loop(0, groups, step, 0)
    keep_ref[...] = acc[pl.ds(0, 16)]
    give_ref[...] = acc[pl.ds(16, 16)].astype(BF16)


def cross_kernel(kept, arrived, feat, sums, forward, back):
    total = kept[pl.ds(0, 2)] + arrived[...].astype(F32)
    sums[...] = total
    back[0] = total[0].astype(BF16)
    back[1] = feat[...]
    forward[...] = total[1].astype(BF16)


def constraint_kernel(
    scale, last, me_ref, sums, forward, back, feat, w_first, bias, w_second, w_third, gain, offset, out, out_t
):
    own = sums[0] + forward[...].astype(F32)
    following = sums[1] + back[0].astype(F32)
    new = node_update(
        jnp.concatenate([feat[...], back[1]], axis=0),
        jnp.concatenate([own, following], axis=0) * scale,
        w_first[...],
        bias[...],
        w_second[...],
        w_third[...],
        gain[...],
        offset[...],
    )
    rows = own.shape[0]
    out[...] = new[:rows]
    out_t[0] = new[:rows].astype(F32).T.astype(BF16)
    turned = new[rows:].astype(F32).T
    out_t[1] = jnp.where(me_ref[0] >= last, jnp.zeros_like(turned), turned).astype(BF16)


def to_columns_kernel(
    scale,
    parts,
    me_ref,
    count_ref,
    col_ref,
    row_ref,
    half_ref,
    feat_ref,
    near_ref,
    far_ref,
    w_first,
    bias,
    w_second,
    w_third,
    gain,
    offset,
    out_ref,
    window,
    acc,
    out_buf,
    table,
    out_sem,
):
    count = count_ref[0]
    groups = (count + GROUP - 1) // GROUP
    my_x, my_y, my_core = place(me_ref[0] % 16)
    for q in range(32):
        x, y, core = place(q % 16)
        table[q] = (core ^ my_core) * 16 + ((my_y - y) & 3) * 4 + (x ^ my_x) * 2 + q // 16
    window[pl.ds(0, 16)] = near_ref[...]
    window[pl.ds(16, 16)] = far_ref[...]
    clear(acc)
    blocks = acc.shape[0] - 1

    def step(group, carry):
        for k in range(GROUP):
            slot = group * GROUP + k
            block = jnp.where(slot < count, col_ref[slot], blocks)
            acc[block] += jnp.dot(window[table[row_ref[slot]]], half_ref[slot], preferred_element_type=F32)
        return carry

    lax.fori_loop(0, groups, step, 0)
    tile = blocks // parts
    copies = []
    for part in range(parts):
        rows = pl.ds(part * tile, tile)
        agg = jnp.concatenate(
            [(acc[part * tile + k] * scale).astype(BF16).T for k in range(tile)], axis=0
        )
        feats = feat_ref[rows].reshape(agg.shape)
        new = node_update(
            feats, agg, w_first[...], bias[...], w_second[...], w_third[...], gain[...], offset[...]
        )
        out_buf[rows] = new.reshape(tile, -1, agg.shape[1])
        copies.append(pltpu.make_async_copy(out_buf.at[rows], out_ref.at[rows], out_sem.at[part]))
        copies[-1].start()
    for copy in copies:
        copy.wait()


SMEM_SPEC = pl.BlockSpec(memory_space=pltpu.SMEM)
VMEM_SPEC = pl.BlockSpec(memory_space=pltpu.VMEM)
HBM_SPEC = pl.BlockSpec(memory_space=pltpu.HBM)


def exchange(array, move):
    bands, cuts = lax.axis_size("band"), lax.axis_size("cuts")
    pairs = []
    for b in range(bands):
        for c in range(cuts):
            to_b, to_x, to_y, to_core = move(b, *place(c))
            if 0 <= to_b < bands:
                pairs.append((b * cuts + c, to_b * cuts + position(to_x, to_y, to_core)))
    return lax.ppermute(array, ("band", "cuts"), pairs)


def in_hbm(array):
    return pltpu.with_memory_space_constraint(array, pltpu.HBM)


def small(mib):
    return pltpu.CompilerParams(vmem_limit_bytes=mib * 1024 * 1024)


def on_device(
    var_feat,
    con_feat,
    slot_column_block,
    slot_constraint_block,
    block_count,
    incidence_coefficients,
    con_first,
    con_bias,
    con_second,
    con_third,
    con_gain,
    con_shift,
    var_first,
    var_bias,
    var_second,
    var_third,
    var_gain,
    var_shift,
):
    width = var_feat.shape[1]
    slots, order = incidence_coefficients.shape[:2]
    blocks = var_feat.shape[0] // order
    groups = slots // GROUP
    columns = var_feat.reshape(blocks, order, width)
    me = lax.axis_index(("band", "cuts")).astype(jnp.int32).reshape(1)
    bands, cuts = lax.axis_size("band"), lax.axis_size("cuts")

    keep, give, half = pl.pallas_call(
        to_constraints_kernel,
        out_shape=(
            jax.ShapeDtypeStruct((16, order, width), F32),
            jax.ShapeDtypeStruct((16, order, width), BF16),
            jax.ShapeDtypeStruct((slots, order, order), BF16),
        ),
        in_specs=[SMEM_SPEC] * 2 + [HBM_SPEC] * 4,
        out_specs=(VMEM_SPEC,) * 3,
        scratch_shapes=[
            pltpu.VMEM((slots, order, order), jnp.int32),
            pltpu.VMEM((blocks, order, width), BF16),
            pltpu.VMEM((33, order, width), F32),
            pltpu.SMEM((32,), jnp.int32),
            pltpu.SMEM((slots,), jnp.int32),
            pltpu.SMEM((slots,), jnp.int32),
            pltpu.SemaphoreType.DMA((groups,)),
            pltpu.SemaphoreType.DMA,
            pltpu.SemaphoreType.DMA((2,)),
        ],
        compiler_params=small(24),
        name="to_constraints",
    )(
        me,
        block_count,
        in_hbm(slot_column_block),
        in_hbm(slot_constraint_block),
        in_hbm(incidence_coefficients),
        in_hbm(columns),
    )

    arrived = exchange(give, lambda b, x, y, c: (b, x, y, 1 - c))
    sums = keep + arrived.astype(F32)
    mine = sums[0:4]
    parts = [sums[4 * k : 4 * k + 4].astype(BF16) for k in (2, 1, 3)]
    came = [
        exchange(part, lambda b, x, y, c, k=k: (b, x, (y + k) % 4, c)) for part, k in zip(parts, (2, 1, 3))
    ]
    for part in came:
        mine = mine + part.astype(F32)
    arrived = exchange(mine[2:4].astype(BF16), lambda b, x, y, c: (b, 1 - x, y, c))
    sums, forward, back = pl.pallas_call(
        cross_kernel,
        out_shape=(
            jax.ShapeDtypeStruct((2, order, width), F32),
            jax.ShapeDtypeStruct((order, width), BF16),
            jax.ShapeDtypeStruct((2, order, width), BF16),
        ),
        in_specs=[VMEM_SPEC] * 3,
        out_specs=(VMEM_SPEC,) * 3,
        compiler_params=small(4),
        name="across_x",
    )(mine, arrived, con_feat)
    back = exchange(back, lambda b, x, y, c: (b - 1, x, y, c))
    forward = exchange(forward, lambda b, x, y, c: (b + 1, x, y, c))

    con_new, turned = pl.pallas_call(
        functools.partial(constraint_kernel, 1.0 / math.sqrt(order * slots), (bands - 1) * cuts),
        out_shape=(
            jax.ShapeDtypeStruct((order, width), BF16),
            jax.ShapeDtypeStruct((2, width, order), BF16),
        ),
        in_specs=[SMEM_SPEC] + [VMEM_SPEC] * 10,
        out_specs=(VMEM_SPEC,) * 2,
        compiler_params=small(8),
        name="constraints",
    )(
        me,
        sums,
        forward,
        back,
        con_feat,
        con_first,
        con_bias.reshape(1, -1),
        con_second,
        con_third,
        con_gain.reshape(1, -1),
        con_shift.reshape(1, -1),
    )

    side = exchange(turned, lambda b, x, y, c: (b, 1 - x, y, c))
    four = jnp.concatenate([turned, side], axis=0)
    others = {k: exchange(four, lambda b, x, y, c, k=k: (b, x, (y + k) % 4, c)) for k in (2, 1, 3)}
    near = jnp.concatenate([four, others[1], others[2], others[3]], axis=0)
    far = exchange(near, lambda b, x, y, c: (b, x, y, 1 - c))

    parts = 1
    var_new = pl.pallas_call(
        functools.partial(to_columns_kernel, 1.0 / math.sqrt(4 * order), parts),
        out_shape=jax.ShapeDtypeStruct((blocks, order, width), BF16),
        in_specs=[SMEM_SPEC] * 4 + [VMEM_SPEC] * 10,
        out_specs=HBM_SPEC,
        scratch_shapes=[
            pltpu.VMEM((32, width, order), BF16),
            pltpu.VMEM((blocks + 1, width, order), F32),
            pltpu.VMEM((blocks, order, width), BF16),
            pltpu.SMEM((32,), jnp.int32),
            pltpu.SemaphoreType.DMA((parts,)),
        ],
        compiler_params=small(32),
        name="to_columns",
    )(
        me,
        block_count,
        slot_column_block,
        slot_constraint_block,
        half,
        columns,
        near,
        far,
        var_first,
        var_bias.reshape(1, -1),
        var_second,
        var_third,
        var_gain.reshape(1, -1),
        var_shift.reshape(1, -1),
    )
    return (con_new, var_new.reshape(var_feat.shape))


def solution(mesh):
    split = P(("band", "cuts"))
    in_specs = (split,) * 6 + (P(),) * 12
    return jax.shard_map(on_device, mesh=mesh, in_specs=in_specs, out_specs=(split, split), check_vma=False)
```

profile of v0, /device:TPU:152, one launch (start us, length us, event | category | flops | bytes accessed | tf_op | source)
XLA Modules:
  0.0 61.0 jit_solution(7970124516514623419)
XLA Ops:
  1.3 5.0 %to_constraints.1 = (f32[16,128,128]{2,1,0:T(8,128)S(1)}, bf16[16,128,128]{2,1,0:T(8,128)(2,1)S(1)}, bf16[160,128,128]{2,1,0:T(8,128)(2,1)S(1)}) custom-call(s32[1]{0:T(128)} %bitcast.me_ref, s32[1]{0:T(128)S(6)} %copy.25.count_ref, s32[160]{0:T(256)} %col_ref.1, s32[160]{0:T(256)} %row_ref.1, s32[160,128,128]{2,1,0:T(8,128)} %coef_hbm.1, ...), custom_call_target="tpu_custom_call" | custom-call | tf_op jit(solution)/shard_map/to_constraints/pallas_call | solution.py:253
  6.5 0.1 collective-permute-start
  6.6 1.9 %collective-permute-done = bf16[16,128,128]{2,1,0:T(8,128)(2,1)S(1)} collective-permute-done((bf16[16,128,128]{2,1,0:T(8,128)(2,1)S(1)}, bf16[16,128,128]{2,1,0:T(8,128)(2,1)S(1)}, u32[]{:S(2)}, u32[]{:S(2)}) %collective-permute-start) | collective-permute-done | bytes 524320 | tf_op jit(solution)/shard_map/ppermute | solution.py:214
  8.5 0.2 fusion.2
  8.7 0.1 collective-permute-start.1
  8.8 0.1 collective-permute-start.3
  8.9 3.2 %collective-permute-start.2 = (bf16[4,128,128]{2,1,0:T(8,128)(2,1)S(1)}, bf16[4,128,128]{2,1,0:T(8,128)(2,1)S(1)}, u32[]{:S(2)}, u32[]{:S(2)}) collective-permute-start(bf16[4,128,128]{2,1,0:T(8,128)(2,1)S(1)} %get-tuple-element.22), channel_id=1, source_target_pairs={{0,2},{1,3},{2,4},{3,5},{4,6},{5,7},{6,0},{7,1},{8,10},{9,11},{10,... | collective-permute-start | bytes 393224 | tf_op jit(solution)/shard_map/ppermute | solution.py:214
  12.1 4.6 %collective-permute-done.1 = bf16[4,128,128]{2,1,0:T(8,128)(2,1)S(1)} collective-permute-done((bf16[4,128,128]{2,1,0:T(8,128)(2,1)S(1)}, bf16[4,128,128]{2,1,0:T(8,128)(2,1)S(1)}, u32[]{:S(2)}, u32[]{:S(2)}) %collective-permute-start.1) | collective-permute-done | bytes 131104 | tf_op jit(solution)/shard_map/ppermute | solution.py:214
  16.7 1.8 %collective-permute-done.3 = bf16[4,128,128]{2,1,0:T(8,128)(2,1)S(1)} collective-permute-done((bf16[4,128,128]{2,1,0:T(8,128)(2,1)S(1)}, bf16[4,128,128]{2,1,0:T(8,128)(2,1)S(1)}, u32[]{:S(2)}, u32[]{:S(2)}) %collective-permute-start.3) | collective-permute-done | bytes 131104 | tf_op jit(solution)/shard_map/ppermute | solution.py:214
  18.6 0.2 collective-permute-start.4
  18.8 4.2 %collective-permute-done.4.arrived = bf16[2,128,128]{2,1,0:T(8,128)(2,1)S(1)} collective-permute-done((bf16[2,128,128]{2,1,0:T(8,128)(2,1)S(1)}, bf16[2,128,128]{2,1,0:T(8,128)(2,1)S(1)}, u32[]{:S(2)}, u32[]{:S(2)}) %collective-permute-start.4) | collective-permute-done | bytes 65568 | tf_op jit(solution)/shard_map/ppermute | solution.py:214
  22.9 4.5 %collective-permute-start.6 = (bf16[2,128,128]{2,1,0:T(8,128)(2,1)S(1)}, bf16[2,128,128]{2,1,0:T(8,128)(2,1)S(1)}, u32[]{:S(2)}, u32[]{:S(2)}) collective-permute-start(bf16[2,128,128]{2,1,0:T(8,128)(2,1)S(1)} %get-tuple-element.14), channel_id=1, source_target_pairs={{16,0},{17,1},{18,2},{19,3},{20,4},{21,5},{22,6},{23,7},{24,8},{25... | collective-permute-start | bytes 196616 | tf_op jit(solution)/shard_map/ppermute | solution.py:214
  27.4 2.9 %collective-permute-start.5 = (bf16[128,128]{1,0:T(8,128)(2,1)S(1)}, bf16[128,128]{1,0:T(8,128)(2,1)S(1)}, u32[]{:S(2)}, u32[]{:S(2)}) collective-permute-start(bf16[128,128]{1,0:T(8,128)(2,1)S(1)} %get-tuple-element.13), channel_id=1, source_target_pairs={{0,16},{1,17},{2,18},{3,19},{4,20},{5,21},{6,22},{7,23},{8,24},{9,... | collective-permute-start | bytes 98312 | tf_op jit(solution)/shard_map/ppermute | solution.py:214
  30.3 6.6 %collective-permute-done.5.forward = bf16[128,128]{1,0:T(8,128)(2,1)S(1)} collective-permute-done((bf16[128,128]{1,0:T(8,128)(2,1)S(1)}, bf16[128,128]{1,0:T(8,128)(2,1)S(1)}, u32[]{:S(2)}, u32[]{:S(2)}) %collective-permute-start.5) | collective-permute-done | bytes 32800 | tf_op jit(solution)/shard_map/ppermute | solution.py:214
  37.0 1.3 %constraints.1 = (bf16[128,128]{1,0:T(8,128)(2,1)}, bf16[2,128,128]{2,1,0:T(8,128)(2,1)S(1)}) custom-call(s32[1]{0:T(128)} %bitcast.me_ref, f32[2,128,128]{2,1,0:T(8,128)S(1)} %get-tuple-element.12.sums, bf16[128,128]{1,0:T(8,128)(2,1)S(1)} %collective-permute-done.5.forward, bf16[2,128,128]{2,1,0:T(8,128)(2,1)S(1)} %collective-permute-done.6.back, ...), custom_call_target="tpu_custom_call" | custom-call | tf_op jit(solution)/shard_map/constraints/pallas_call | solution.py:309
  38.3 4.2 %collective-permute-done.7 = bf16[2,128,128]{2,1,0:T(8,128)(2,1)S(1)} collective-permute-done((bf16[2,128,128]{2,1,0:T(8,128)(2,1)S(1)}, bf16[2,128,128]{2,1,0:T(8,128)(2,1)S(1)}, u32[]{:S(2)}, u32[]{:S(2)}) %collective-permute-start.7) | collective-permute-done | bytes 65568 | tf_op jit(solution)/shard_map/ppermute | solution.py:214
  42.6 0.8 %collective-permute-start.8 = (bf16[4,128,128]{2,1,0:T(8,128)(2,1)S(1)}, bf16[4,128,128]{2,1,0:T(8,128)(2,1)S(1)}, u32[]{:S(2)}, u32[]{:S(2)}) collective-permute-start(bf16[4,128,128]{2,1,0:T(8,128)(2,1)S(1)} %get-tuple-element.23), channel_id=1, source_target_pairs={{0,2},{1,3},{2,4},{3,5},{4,6},{5,7},{6,0},{7,1},{8,10},{9,11},{10,... | collective-permute-start | bytes 393224 | tf_op jit(solution)/shard_map/ppermute | solution.py:214
  43.3 1.9 %collective-permute-start.9 = (bf16[4,128,128]{2,1,0:T(8,128)(2,1)S(1)}, bf16[4,128,128]{2,1,0:T(8,128)(2,1)S(1)}, u32[]{:S(2)}, u32[]{:S(2)}) collective-permute-start(bf16[4,128,128]{2,1,0:T(8,128)(2,1)S(1)} %get-tuple-element.23), channel_id=1, source_target_pairs={{0,4},{1,5},{2,6},{3,7},{4,0},{5,1},{6,2},{7,3},{8,12},{9,13},{10,... | collective-permute-start | bytes 393224 | tf_op jit(solution)/shard_map/ppermute | solution.py:214
  45.2 2.3 %collective-permute-done.8 = bf16[4,128,128]{2,1,0:T(8,128)(2,1)S(1)} collective-permute-done((bf16[4,128,128]{2,1,0:T(8,128)(2,1)S(1)}, bf16[4,128,128]{2,1,0:T(8,128)(2,1)S(1)}, u32[]{:S(2)}, u32[]{:S(2)}) %collective-permute-start.8) | collective-permute-done | bytes 131104 | tf_op jit(solution)/shard_map/ppermute | solution.py:214
  47.6 2.2 %collective-permute-done.9 = bf16[4,128,128]{2,1,0:T(8,128)(2,1)S(1)} collective-permute-done((bf16[4,128,128]{2,1,0:T(8,128)(2,1)S(1)}, bf16[4,128,128]{2,1,0:T(8,128)(2,1)S(1)}, u32[]{:S(2)}, u32[]{:S(2)}) %collective-permute-start.9) | collective-permute-done | bytes 131104 | tf_op jit(solution)/shard_map/ppermute | solution.py:214
  49.8 1.6 %collective-permute-done.10 = bf16[4,128,128]{2,1,0:T(8,128)(2,1)S(1)} collective-permute-done((bf16[4,128,128]{2,1,0:T(8,128)(2,1)S(1)}, bf16[4,128,128]{2,1,0:T(8,128)(2,1)S(1)}, u32[]{:S(2)}, u32[]{:S(2)}) %collective-permute-start.10) | collective-permute-done | bytes 131104 | tf_op jit(solution)/shard_map/ppermute | solution.py:214
  51.4 0.1 collective-permute-start.11
  51.5 1.9 %collective-permute-done.11.far_ref = bf16[16,128,128]{2,1,0:T(8,128)(2,1)S(1)} collective-permute-done((bf16[16,128,128]{2,1,0:T(8,128)(2,1)S(1)}, bf16[16,128,128]{2,1,0:T(8,128)(2,1)S(1)}, u32[]{:S(2)}, u32[]{:S(2)}) %collective-permute-start.11) | collective-permute-done | bytes 524320 | tf_op jit(solution)/shard_map/ppermute | solution.py:214
  53.5 7.5 %to_columns.1 = bf16[40,128,128]{2,1,0:T(8,128)(2,1)} custom-call(s32[1]{0:T(128)} %bitcast.me_ref, s32[1]{0:T(128)S(6)} %copy.25.count_ref, s32[160]{0:T(256)S(1)} %copy-done.8, s32[160]{0:T(256)S(1)} %copy-done.9, bf16[160,128,128]{2,1,0:T(8,128)(2,1)S(1)} %get-tuple-element.16.half_ref, bf16[40,128,128]{2,1,0:T(8,128)(2,1)S(1)} %bitcast.10, ...), custom_call_target="tpu_custom_call" | custom-call | tf_op jit(solution)/shard_map/to_columns/pallas_call | solution.py:340
  (45 shorter events, 0.3 us)
Async XLA Ops:
  6.3 30.6 %copy-start.3 = (bf16[256,256]{1,0:T(8,128)(2,1)S(1)}, bf16[256,256]{1,0:T(8,128)(2,1)}, u32[]{:S(2)}) copy-start(bf16[256,256]{1,0:T(8,128)(2,1)} %w_first.2) | copy-start | bytes 393220
  6.3 30.6 %copy-start.4 = (bf16[256,256]{1,0:T(8,128)(2,1)S(1)}, bf16[256,256]{1,0:T(8,128)(2,1)}, u32[]{:S(2)}) copy-start(bf16[256,256]{1,0:T(8,128)(2,1)} %w_second.2) | copy-start | bytes 393220
  6.3 30.6 %copy-start.7 = (bf16[256,128]{1,0:T(8,128)(2,1)S(1)}, bf16[256,128]{1,0:T(8,128)(2,1)}, u32[]{:S(2)}) copy-start(bf16[256,128]{1,0:T(8,128)(2,1)} %w_third.2) | copy-start | bytes 196612
  6.4 47.1 %copy-start = (bf16[5120,128]{1,0:T(8,128)(2,1)S(1)}, bf16[5120,128]{1,0:T(8,128)(2,1)}, u32[]{:S(2)}) copy-start(bf16[5120,128]{1,0:T(8,128)(2,1)} %param.18) | copy-start | bytes 3932164
  6.4 47.0 %copy-start.1 = (bf16[256,256]{1,0:T(8,128)(2,1)S(1)}, bf16[256,256]{1,0:T(8,128)(2,1)}, u32[]{:S(2)}) copy-start(bf16[256,256]{1,0:T(8,128)(2,1)} %w_first.3) | copy-start | bytes 393220
  6.4 47.0 %copy-start.2 = (bf16[256,256]{1,0:T(8,128)(2,1)S(1)}, bf16[256,256]{1,0:T(8,128)(2,1)}, u32[]{:S(2)}) copy-start(bf16[256,256]{1,0:T(8,128)(2,1)} %w_second.3) | copy-start | bytes 393220
  6.4 47.0 %copy-start.6 = (bf16[256,128]{1,0:T(8,128)(2,1)S(1)}, bf16[256,128]{1,0:T(8,128)(2,1)}, u32[]{:S(2)}) copy-start(bf16[256,128]{1,0:T(8,128)(2,1)} %w_third.3) | copy-start | bytes 196612
  6.4 47.0 %copy-start.8 = (s32[160]{0:T(256)S(1)}, s32[160]{0:T(256)}, u32[]{:S(2)}) copy-start(s32[160]{0:T(256)} %col_ref.1) | copy-start | bytes 1924
  6.5 47.0 %copy-start.9 = (s32[160]{0:T(256)S(1)}, s32[160]{0:T(256)}, u32[]{:S(2)}) copy-start(s32[160]{0:T(256)} %row_ref.1) | copy-start | bytes 1924
  6.5 47.0 %copy-start.11 = (f32[256]{0:T(256)S(1)}, f32[256]{0:T(256)}, u32[]{:S(2)}) copy-start(f32[256]{0:T(256)} %param.31) | copy-start | bytes 3076
  6.5 47.0 %copy-start.12 = (f32[128]{0:T(128)S(1)}, f32[128]{0:T(128)}, u32[]{:S(2)}) copy-start(f32[128]{0:T(128)} %param.34) | copy-start | bytes 1540
  6.5 47.0 %copy-start.13 = (f32[128]{0:T(128)S(1)}, f32[128]{0:T(128)}, u32[]{:S(2)}) copy-start(f32[128]{0:T(128)} %param.35) | copy-start | bytes 1540
  6.5 2.0 %collective-permute-start = (bf16[16,128,128]{2,1,0:T(8,128)(2,1)S(1)}, bf16[16,128,128]{2,1,0:T(8,128)(2,1)S(1)}, u32[]{:S(2)}, u32[]{:S(2)}) collective-permute-start(bf16[16,128,128]{2,1,0:T(8,128)(2,1)S(1)} %get-tuple-element.11), channel_id=1, source_target_pairs={{0,1},{1,0},{2,3},{3,2},{4,5},{5,4},{6,7},{7,6},{8,9},{9,8},{10,11... | collective-permute-start | bytes 1572872 | tf_op jit(solution)/shard_map/ppermute | solution.py:214
  8.7 8.0 %collective-permute-start.1 = (bf16[4,128,128]{2,1,0:T(8,128)(2,1)S(1)}, bf16[4,128,128]{2,1,0:T(8,128)(2,1)S(1)}, u32[]{:S(2)}, u32[]{:S(2)}) collective-permute-start(bf16[4,128,128]{2,1,0:T(8,128)(2,1)S(1)} %get-tuple-element.20), channel_id=1, source_target_pairs={{0,4},{1,5},{2,6},{3,7},{4,0},{5,1},{6,2},{7,3},{8,12},{9,13},{10,... | collective-permute-start | bytes 393224 | tf_op jit(solution)/shard_map/ppermute | solution.py:214
  8.8 9.6 %collective-permute-start.3 = (bf16[4,128,128]{2,1,0:T(8,128)(2,1)S(1)}, bf16[4,128,128]{2,1,0:T(8,128)(2,1)S(1)}, u32[]{:S(2)}, u32[]{:S(2)}) collective-permute-start(bf16[4,128,128]{2,1,0:T(8,128)(2,1)S(1)} %get-tuple-element.21), channel_id=1, source_target_pairs={{0,6},{1,7},{2,0},{3,1},{4,2},{5,3},{6,4},{7,5},{8,14},{9,15},{10,... | collective-permute-start | bytes 393224 | tf_op jit(solution)/shard_map/ppermute | solution.py:214
  8.9 9.5 %collective-permute-start.2 = (bf16[4,128,128]{2,1,0:T(8,128)(2,1)S(1)}, bf16[4,128,128]{2,1,0:T(8,128)(2,1)S(1)}, u32[]{:S(2)}, u32[]{:S(2)}) collective-permute-start(bf16[4,128,128]{2,1,0:T(8,128)(2,1)S(1)} %get-tuple-element.22), channel_id=1, source_target_pairs={{0,2},{1,3},{2,4},{3,5},{4,6},{5,7},{6,0},{7,1},{8,10},{9,11},{10,... | collective-permute-start | bytes 393224 | tf_op jit(solution)/shard_map/ppermute | solution.py:214
  18.6 4.4 %collective-permute-start.4 = (bf16[2,128,128]{2,1,0:T(8,128)(2,1)S(1)}, bf16[2,128,128]{2,1,0:T(8,128)(2,1)S(1)}, u32[]{:S(2)}, u32[]{:S(2)}) collective-permute-start(bf16[2,128,128]{2,1,0:T(8,128)(2,1)S(1)} %slice.35), channel_id=1, source_target_pairs={{0,8},{1,9},{2,10},{3,11},{4,12},{5,13},{6,14},{7,15},{8,0},{9,1},... | collective-permute-start | bytes 196616 | tf_op jit(solution)/shard_map/ppermute | solution.py:214
  22.9 14.0 %collective-permute-start.6 = (bf16[2,128,128]{2,1,0:T(8,128)(2,1)S(1)}, bf16[2,128,128]{2,1,0:T(8,128)(2,1)S(1)}, u32[]{:S(2)}, u32[]{:S(2)}) collective-permute-start(bf16[2,128,128]{2,1,0:T(8,128)(2,1)S(1)} %get-tuple-element.14), channel_id=1, source_target_pairs={{16,0},{17,1},{18,2},{19,3},{20,4},{21,5},{22,6},{23,7},{24,8},{25... | collective-permute-start | bytes 196616 | tf_op jit(solution)/shard_map/ppermute | solution.py:214
  27.4 9.5 %collective-permute-start.5 = (bf16[128,128]{1,0:T(8,128)(2,1)S(1)}, bf16[128,128]{1,0:T(8,128)(2,1)S(1)}, u32[]{:S(2)}, u32[]{:S(2)}) collective-permute-start(bf16[128,128]{1,0:T(8,128)(2,1)S(1)} %get-tuple-element.13), channel_id=1, source_target_pairs={{0,16},{1,17},{2,18},{3,19},{4,20},{5,21},{6,22},{7,23},{8,24},{9,... | collective-permute-start | bytes 98312 | tf_op jit(solution)/shard_map/ppermute | solution.py:214
  38.3 4.3 %collective-permute-start.7 = (bf16[2,128,128]{2,1,0:T(8,128)(2,1)S(1)}, bf16[2,128,128]{2,1,0:T(8,128)(2,1)S(1)}, u32[]{:S(2)}, u32[]{:S(2)}) collective-permute-start(bf16[2,128,128]{2,1,0:T(8,128)(2,1)S(1)} %get-tuple-element.17), channel_id=1, source_target_pairs={{0,8},{1,9},{2,10},{3,11},{4,12},{5,13},{6,14},{7,15},{8,0},{9,1},... | collective-permute-start | bytes 196616 | tf_op jit(solution)/shard_map/ppermute | solution.py:214
  42.6 5.0 %collective-permute-start.8 = (bf16[4,128,128]{2,1,0:T(8,128)(2,1)S(1)}, bf16[4,128,128]{2,1,0:T(8,128)(2,1)S(1)}, u32[]{:S(2)}, u32[]{:S(2)}) collective-permute-start(bf16[4,128,128]{2,1,0:T(8,128)(2,1)S(1)} %get-tuple-element.23), channel_id=1, source_target_pairs={{0,2},{1,3},{2,4},{3,5},{4,6},{5,7},{6,0},{7,1},{8,10},{9,11},{10,... | collective-permute-start | bytes 393224 | tf_op jit(solution)/shard_map/ppermute | solution.py:214
  43.3 6.5 %collective-permute-start.9 = (bf16[4,128,128]{2,1,0:T(8,128)(2,1)S(1)}, bf16[4,128,128]{2,1,0:T(8,128)(2,1)S(1)}, u32[]{:S(2)}, u32[]{:S(2)}) collective-permute-start(bf16[4,128,128]{2,1,0:T(8,128)(2,1)S(1)} %get-tuple-element.23), channel_id=1, source_target_pairs={{0,4},{1,5},{2,6},{3,7},{4,0},{5,1},{6,2},{7,3},{8,12},{9,13},{10,... | collective-permute-start | bytes 393224 | tf_op jit(solution)/shard_map/ppermute | solution.py:214
  45.2 6.2 %collective-permute-start.10 = (bf16[4,128,128]{2,1,0:T(8,128)(2,1)S(1)}, bf16[4,128,128]{2,1,0:T(8,128)(2,1)S(1)}, u32[]{:S(2)}, u32[]{:S(2)}) collective-permute-start(bf16[4,128,128]{2,1,0:T(8,128)(2,1)S(1)} %get-tuple-element.23), channel_id=1, source_target_pairs={{0,6},{1,7},{2,0},{3,1},{4,2},{5,3},{6,4},{7,5},{8,14},{9,15},{10,... | collective-permute-start | bytes 393224 | tf_op jit(solution)/shard_map/ppermute | solution.py:214
  51.4 2.0 %collective-permute-start.11 = (bf16[16,128,128]{2,1,0:T(8,128)(2,1)S(1)}, bf16[16,128,128]{2,1,0:T(8,128)(2,1)S(1)}, u32[]{:S(2)}, u32[]{:S(2)}) collective-permute-start(bf16[16,128,128]{2,1,0:T(8,128)(2,1)S(1)} %constant_dynamic-update-slice_fusion.2.near_ref), channel_id=1, source_target_pairs={{0,1},{1,0},{2,3},{3,2},{4,5},{5,4},{6,7},{7,6},{8,9},{9,8},{10,11... | collective-permute-start | bytes 1572872 | tf_op jit(solution)/shard_map/ppermute | solution.py:214
  (4 other events, 113.5 us)
where the time goes:
time: 61.2 us; the launch traced here: 61 us
  waiting for transfers between devices  31.3 us (51%)
  Pallas kernels  13.8 us (23%)
  starting transfers between devices  13.8 us (23%)
  between operations  1.61 us (3%)
    ppermute x12, waiting for transfers between devices, exchange(): return lax.ppermute(array, ('band', 'cuts'), pairs)  31.3 us
    ppermute x12, starting transfers between devices, exchange(): return lax.ppermute(array, ('band', 'cuts'), pairs)  13.8 us
    pallas_call x1, Pallas kernels, on_device(): pl.pallas_call(functools.partial(to_columns_kernel, 1.0 / math.sqrt(4 * o...  7.52 us
    pallas_call x1, Pallas kernels, on_device(): pl.pallas_call(to_constraints_kernel, out_shape=(jax.ShapeDtypeStruct((16...  5.02 us
    pallas_call x1, Pallas kernels, on_device(): pl.pallas_call(functools.partial(constraint_kernel, 1.0 / math.sqrt(order...  1.26 us
  transfers between devices with their start and end apart: 12, of which 10 were waited for; matrix products, arithmetic and copies ran while one was open for 0% of the time, Pallas kernels for 0%

commit v1 on v0

--- a/solution.py
+++ b/solution.py
@@ -12,6 +12,7 @@
 F32 = jnp.float32
 BF16 = jnp.bfloat16
 GROUP = 16
+COLUMN_GROUP = 40
 
 
 def place(index):
@@ -30,8 +31,8 @@
 
 def node_update(feats, scaled_agg, w_first, bias, w_second, w_third, gain, offset):
     joined = jnp.concatenate([feats, scaled_agg.astype(BF16)], axis=1)
-    hidden = jnp.maximum(jnp.dot(joined, w_first, preferred_element_type=F32) + bias, 0.0).astype(BF16)
-    middle = jnp.maximum(jnp.dot(hidden, w_second, preferred_element_type=F32), 0.0).astype(BF16)
+    hidden = jnp.maximum((jnp.dot(joined, w_first, preferred_element_type=F32) + bias).astype(BF16), 0)
+    middle = jnp.maximum(jnp.dot(hidden, w_second, preferred_element_type=F32).astype(BF16), 0)
     output = jnp.dot(middle, w_third, preferred_element_type=F32)
     return layer_norm(feats.astype(F32) + output, gain, offset).astype(BF16)
 
@@ -80,13 +81,12 @@
     feat_copy = pltpu.make_async_copy(feat_hbm, feat_buf, feat_sem)
     col_copy.start()
     row_copy.start()
-    coefficients(0).start()
     feat_copy.start()
-    lax.fori_loop(1, groups, start, 0)
-    my_x, my_y, my_core = place(me_ref[0] % 16)
+    lax.fori_loop(0, groups, start, 0)
+    my_core = me_ref[0] % 2
     for q in range(32):
         x, y, core = place(q % 16)
-        table[q] = (core ^ my_core) * 16 + ((y - my_y) & 3) * 4 + (x ^ my_x) * 2 + q // 16
+        table[q] = (core ^ my_core) * 16 + (x ^ (q // 16)) * 8 + y * 2 + q // 16
     clear(acc)
     col_copy.wait()
     row_copy.wait()
@@ -107,21 +107,28 @@
     give_ref[...] = acc[pl.ds(16, 16)].astype(BF16)
 
 
-def cross_kernel(kept, arrived, feat, sums, forward, back):
-    total = kept[pl.ds(0, 2)] + arrived[...].astype(F32)
+def cross_kernel(me_ref, arrived, feat, sums, even, odd):
+    total = arrived[0].astype(F32)
+    for chip in range(1, arrived.shape[0]):
+        total = total + arrived[chip].astype(F32)
     sums[...] = total
-    back[0] = total[0].astype(BF16)
-    back[1] = feat[...]
-    forward[...] = total[1].astype(BF16)
+    lower = me_ref[0] // 16 % 2 == 0
+    even[0] = jnp.where(lower, total[1], total[0]).astype(BF16)
+    odd[0] = jnp.where(lower, total[0], total[1]).astype(BF16)
+    even[1] = feat[...]
+    odd[1] = feat[...]
 
 
 def constraint_kernel(
-    scale, last, me_ref, sums, forward, back, feat, w_first, bias, w_second, w_third, gain, offset, out, out_t
+    scale, last, me_ref, sums, odd, even, feat, w_first, bias, w_second, w_third, gain, offset, out, out_t
 ):
-    own = sums[0] + forward[...].astype(F32)
-    following = sums[1] + back[0].astype(F32)
+    lower = me_ref[0] // 16 % 2 == 0
+    first, second = even[0].astype(F32), odd[0].astype(F32)
+    next_feat = jnp.where(lower, even[1], odd[1])
+    own = sums[0] + jnp.where(lower, second, first)
+    following = sums[1] + jnp.where(lower, first, second)
     new = node_update(
-        jnp.concatenate([feat[...], back[1]], axis=0),
+        jnp.concatenate([feat[...], next_feat], axis=0),
         jnp.concatenate([own, following], axis=0) * scale,
         w_first[...],
         bias[...],
@@ -162,24 +169,23 @@
     out_sem,
 ):
     count = count_ref[0]
-    groups = (count + GROUP - 1) // GROUP
     my_x, my_y, my_core = place(me_ref[0] % 16)
     for q in range(32):
         x, y, core = place(q % 16)
-        table[q] = (core ^ my_core) * 16 + ((my_y - y) & 3) * 4 + (x ^ my_x) * 2 + q // 16
+        table[q] = (core ^ my_core) * 16 + ((my_y - y) & 3) * 4 + (x ^ my_x ^ (q // 16)) * 2 + q // 16
     window[pl.ds(0, 16)] = near_ref[...]
     window[pl.ds(16, 16)] = far_ref[...]
     clear(acc)
     blocks = acc.shape[0] - 1
 
     def step(group, carry):
-        for k in range(GROUP):
-            slot = group * GROUP + k
+        for k in range(COLUMN_GROUP):
+            slot = group * COLUMN_GROUP + k
             block = jnp.where(slot < count, col_ref[slot], blocks)
             acc[block] += jnp.dot(window[table[row_ref[slot]]], half_ref[slot], preferred_element_type=F32)
         return carry
 
-    lax.fori_loop(0, groups, step, 0)
+    lax.fori_loop(0, (count + COLUMN_GROUP - 1) // COLUMN_GROUP, step, 0)
     tile = blocks // parts
     copies = []
     for part in range(parts):
@@ -282,29 +288,23 @@
     )
 
     arrived = exchange(give, lambda b, x, y, c: (b, x, y, 1 - c))
-    sums = keep + arrived.astype(F32)
-    mine = sums[0:4]
-    parts = [sums[4 * k : 4 * k + 4].astype(BF16) for k in (2, 1, 3)]
-    came = [
-        exchange(part, lambda b, x, y, c, k=k: (b, x, (y + k) % 4, c)) for part, k in zip(parts, (2, 1, 3))
-    ]
-    for part in came:
-        mine = mine + part.astype(F32)
-    arrived = exchange(mine[2:4].astype(BF16), lambda b, x, y, c: (b, 1 - x, y, c))
-    sums, forward, back = pl.pallas_call(
+    sums = (keep + arrived.astype(F32)).astype(BF16).reshape(8, 2, order, width)
+    same_core = [[position(x, y, core) for x in range(2) for y in range(4)] for core in range(2)]
+    arrived = lax.all_to_all(sums, "cuts", 0, 0, tiled=True, axis_index_groups=same_core)
+    sums, even, odd = pl.pallas_call(
         cross_kernel,
         out_shape=(
             jax.ShapeDtypeStruct((2, order, width), F32),
-            jax.ShapeDtypeStruct((order, width), BF16),
+            jax.ShapeDtypeStruct((2, order, width), BF16),
             jax.ShapeDtypeStruct((2, order, width), BF16),
         ),
-        in_specs=[VMEM_SPEC] * 3,
+        in_specs=[SMEM_SPEC] + [VMEM_SPEC] * 2,
         out_specs=(VMEM_SPEC,) * 3,
-        compiler_params=small(4),
+        compiler_params=small(8),
         name="across_x",
-    )(mine, arrived, con_feat)
-    back = exchange(back, lambda b, x, y, c: (b - 1, x, y, c))
-    forward = exchange(forward, lambda b, x, y, c: (b + 1, x, y, c))
+    )(me, arrived, con_feat)
+    odd = exchange(odd, lambda b, x, y, c: (((b + 1) ^ 1) - 1, 1 - x, y, c))
+    even = exchange(even, lambda b, x, y, c: (b ^ 1, 1 - x, y, c))
 
     con_new, turned = pl.pallas_call(
         functools.partial(constraint_kernel, 1.0 / math.sqrt(order * slots), (bands - 1) * cuts),
@@ -319,8 +319,8 @@
     )(
         me,
         sums,
-        forward,
-        back,
+        odd,
+        even,
         con_feat,
         con_first,
         con_bias.reshape(1, -1),
@@ -336,7 +336,7 @@
     near = jnp.concatenate([four, others[1], others[2], others[3]], axis=0)
     far = exchange(near, lambda b, x, y, c: (b, x, y, 1 - c))
 
-    parts = 1
+    parts = 4
     var_new = pl.pallas_call(
         functools.partial(to_columns_kernel, 1.0 / math.sqrt(4 * order), parts),
         out_shape=jax.ShapeDtypeStruct((blocks, order, width), BF16),

time: 61.2 us -> 56.3 us (0.920)
  the two profiles are of different devices: /device:TPU:152 before, /device:TPU:193 now
where the time goes in v1:
time: 56.3 us; the launch traced here: 55.3 us
  starting transfers between devices  16 us (28%)
  Pallas kernels  13 us (23%)
  blocking collectives  12.9 us (23%)
  waiting for transfers between devices  11.5 us (20%)
  between operations  1.55 us (3%)
    ppermute x8, starting transfers between devices, exchange(): return lax.ppermute(array, ('band', 'cuts'), pairs)  16 us
    all_to_all x1, blocking collectives, on_device(): lax.all_to_all(sums, 'cuts', 0, 0, tiled=True, axis_index_groups=same_core)  12.9 us
    ppermute x8, waiting for transfers between devices, exchange(): return lax.ppermute(array, ('band', 'cuts'), pairs)  11.5 us
    pallas_call x1, Pallas kernels, on_device(): pl.pallas_call(functools.partial(to_columns_kernel, 1.0 / math.sqrt(4 * o...  6.55 us
    pallas_call x1, Pallas kernels, on_device(): pl.pallas_call(to_constraints_kernel, out_shape=(jax.ShapeDtypeStruct((16...  5.13 us
    pallas_call x1, Pallas kernels, on_device(): pl.pallas_call(functools.partial(constraint_kernel, 1.0 / math.sqrt(order...  1.26 us
  transfers between devices with their start and end apart: 8, of which 7 were waited for; matrix products, arithmetic and copies ran while one was open for 0% of the time, Pallas kernels for 0%

profile of v1, /device:TPU:193, one launch (start us, length us, event | category | flops | bytes accessed | tf_op | source)
XLA Modules:
  0.0 55.3 jit_solution(14180643837997342857)
XLA Ops:
  1.4 5.1 %to_constraints.1 = (f32[16,128,128]{2,1,0:T(8,128)S(1)}, bf16[16,128,128]{2,1,0:T(8,128)(2,1)S(1)}, bf16[160,128,128]{2,1,0:T(8,128)(2,1)S(1)}) custom-call(s32[1]{0:T(128)} %bitcast.me_ref, s32[1]{0:T(128)S(6)} %copy.25.count_ref, s32[160]{0:T(256)} %col_ref.1, s32[160]{0:T(256)} %row_ref.1, s32[160,128,128]{2,1,0:T(8,128)} %coef_hbm.1, ...), custom_call_target="tpu_custom_call" | custom-call | tf_op jit(solution)/shard_map/to_constraints/pallas_call | solution.py:259
  6.5 0.0 copy-start
  6.5 0.0 copy-start.6
  6.5 0.0 copy-start.8
  6.6 0.1 collective-permute-start
  6.7 1.9 %collective-permute-done = bf16[16,128,128]{2,1,0:T(8,128)(2,1)S(1)} collective-permute-done((bf16[16,128,128]{2,1,0:T(8,128)(2,1)S(1)}, bf16[16,128,128]{2,1,0:T(8,128)(2,1)S(1)}, u32[]{:S(2)}, u32[]{:S(2)}) %collective-permute-start) | collective-permute-done | bytes 524320 | tf_op jit(solution)/shard_map/ppermute | solution.py:220
  8.6 0.1 add_convert_fusion
  8.7 12.9 %all_to_all.5.arrived = bf16[8,2,128,128]{3,2,1,0:T(8,128)(2,1)S(1)} all-to-all(bf16[8,2,128,128]{3,2,1,0:T(8,128)(2,1)S(1)} %bitcast.18), channel_id=1, replica_groups={{0,2,4,6,8,10,12,14},{1,3,5,7,9,11,13,15},{16,18,20,22,24,26,28,30},{17..., dimensions={0} | all-to-all | bytes 1048576 | tf_op jit(solution)/shard_map/all_to_all | solution.py:293
  21.7 0.1 across_x.1
  21.7 3.6 %collective-permute-start.1 = (bf16[2,128,128]{2,1,0:T(8,128)(2,1)S(1)}, bf16[2,128,128]{2,1,0:T(8,128)(2,1)S(1)}, u32[]{:S(2)}, u32[]{:S(2)}) collective-permute-start(bf16[2,128,128]{2,1,0:T(8,128)(2,1)S(1)} %get-tuple-element.13), channel_id=1, source_target_pairs={{16,40},{17,41},{18,42},{19,43},{20,44},{21,45},{22,46},{23,47},{2... | collective-permute-start | bytes 196616 | tf_op jit(solution)/shard_map/ppermute | solution.py:220
  25.3 2.3 %collective-permute-start.2 = (bf16[2,128,128]{2,1,0:T(8,128)(2,1)S(1)}, bf16[2,128,128]{2,1,0:T(8,128)(2,1)S(1)}, u32[]{:S(2)}, u32[]{:S(2)}) collective-permute-start(bf16[2,128,128]{2,1,0:T(8,128)(2,1)S(1)} %get-tuple-element.14), channel_id=1, source_target_pairs={{0,24},{1,25},{2,26},{3,27},{4,28},{5,29},{6,30},{7,31},{8,16},{9,... | collective-permute-start | bytes 196616 | tf_op jit(solution)/shard_map/ppermute | solution.py:220
  27.6 1.2 %collective-permute-done.1.odd = bf16[2,128,128]{2,1,0:T(8,128)(2,1)S(1)} collective-permute-done((bf16[2,128,128]{2,1,0:T(8,128)(2,1)S(1)}, bf16[2,128,128]{2,1,0:T(8,128)(2,1)S(1)}, u32[]{:S(2)}, u32[]{:S(2)}) %collective-permute-start.1) | collective-permute-done | bytes 65568 | tf_op jit(solution)/shard_map/ppermute | solution.py:220
  28.8 0.9 %collective-permute-done.2.even = bf16[2,128,128]{2,1,0:T(8,128)(2,1)S(1)} collective-permute-done((bf16[2,128,128]{2,1,0:T(8,128)(2,1)S(1)}, bf16[2,128,128]{2,1,0:T(8,128)(2,1)S(1)}, u32[]{:S(2)}, u32[]{:S(2)}) %collective-permute-start.2) | collective-permute-done | bytes 65568 | tf_op jit(solution)/shard_map/ppermute | solution.py:220
  29.8 1.3 %constraints.1 = (bf16[128,128]{1,0:T(8,128)(2,1)}, bf16[2,128,128]{2,1,0:T(8,128)(2,1)S(1)}) custom-call(s32[1]{0:T(128)} %bitcast.me_ref, f32[2,128,128]{2,1,0:T(8,128)S(1)} %get-tuple-element.12.sums, bf16[2,128,128]{2,1,0:T(8,128)(2,1)S(1)} %collective-permute-done.1.odd, bf16[2,128,128]{2,1,0:T(8,128)(2,1)S(1)} %collective-permute-done.2.even, ...), custom_call_target="tpu_custom_call" | custom-call | tf_op jit(solution)/shard_map/constraints/pallas_call | solution.py:309
  31.1 3.1 %collective-permute-done.3 = bf16[2,128,128]{2,1,0:T(8,128)(2,1)S(1)} collective-permute-done((bf16[2,128,128]{2,1,0:T(8,128)(2,1)S(1)}, bf16[2,128,128]{2,1,0:T(8,128)(2,1)S(1)}, u32[]{:S(2)}, u32[]{:S(2)}) %collective-permute-start.3) | collective-permute-done | bytes 65568 | tf_op jit(solution)/shard_map/ppermute | solution.py:220
  34.2 2.5 %collective-permute-start.4 = (bf16[4,128,128]{2,1,0:T(8,128)(2,1)S(1)}, bf16[4,128,128]{2,1,0:T(8,128)(2,1)S(1)}, u32[]{:S(2)}, u32[]{:S(2)}) collective-permute-start(bf16[4,128,128]{2,1,0:T(8,128)(2,1)S(1)} %get-tuple-element.18), channel_id=1, source_target_pairs={{0,2},{1,3},{2,4},{3,5},{4,6},{5,7},{6,0},{7,1},{8,10},{9,11},{10,... | collective-permute-start | bytes 393224 | tf_op jit(solution)/shard_map/ppermute | solution.py:220
  36.6 1.8 %collective-permute-start.5 = (bf16[4,128,128]{2,1,0:T(8,128)(2,1)S(1)}, bf16[4,128,128]{2,1,0:T(8,128)(2,1)S(1)}, u32[]{:S(2)}, u32[]{:S(2)}) collective-permute-start(bf16[4,128,128]{2,1,0:T(8,128)(2,1)S(1)} %get-tuple-element.18), channel_id=1, source_target_pairs={{0,4},{1,5},{2,6},{3,7},{4,0},{5,1},{6,2},{7,3},{8,12},{9,13},{10,... | collective-permute-start | bytes 393224 | tf_op jit(solution)/shard_map/ppermute | solution.py:220
  38.4 0.8 %collective-permute-start.6 = (bf16[4,128,128]{2,1,0:T(8,128)(2,1)S(1)}, bf16[4,128,128]{2,1,0:T(8,128)(2,1)S(1)}, u32[]{:S(2)}, u32[]{:S(2)}) collective-permute-start(bf16[4,128,128]{2,1,0:T(8,128)(2,1)S(1)} %get-tuple-element.18), channel_id=1, source_target_pairs={{0,6},{1,7},{2,0},{3,1},{4,2},{5,3},{6,4},{7,5},{8,14},{9,15},{10,... | collective-permute-start | bytes 393224 | tf_op jit(solution)/shard_map/ppermute | solution.py:220
  39.3 0.3 collective-permute-done.4
  39.6 2.6 %collective-permute-done.5 = bf16[4,128,128]{2,1,0:T(8,128)(2,1)S(1)} collective-permute-done((bf16[4,128,128]{2,1,0:T(8,128)(2,1)S(1)}, bf16[4,128,128]{2,1,0:T(8,128)(2,1)S(1)}, u32[]{:S(2)}, u32[]{:S(2)}) %collective-permute-start.5) | collective-permute-done | bytes 131104 | tf_op jit(solution)/shard_map/ppermute | solution.py:220
  42.2 0.0 collective-permute-done.6
  42.3 4.9 %collective-permute-start.7 = (bf16[16,128,128]{2,1,0:T(8,128)(2,1)S(1)}, bf16[16,128,128]{2,1,0:T(8,128)(2,1)S(1)}, u32[]{:S(2)}, u32[]{:S(2)}) collective-permute-start(bf16[16,128,128]{2,1,0:T(8,128)(2,1)S(1)} %constant_dynamic-update-slice_fusion.2.near_ref), channel_id=1, source_target_pairs={{0,1},{1,0},{2,3},{3,2},{4,5},{5,4},{6,7},{7,6},{8,9},{9,8},{10,11... | collective-permute-start | bytes 1572872 | tf_op jit(solution)/shard_map/ppermute | solution.py:220
  47.2 1.5 %collective-permute-done.7.far_ref = bf16[16,128,128]{2,1,0:T(8,128)(2,1)S(1)} collective-permute-done((bf16[16,128,128]{2,1,0:T(8,128)(2,1)S(1)}, bf16[16,128,128]{2,1,0:T(8,128)(2,1)S(1)}, u32[]{:S(2)}, u32[]{:S(2)}) %collective-permute-start.7) | collective-permute-done | bytes 524320 | tf_op jit(solution)/shard_map/ppermute | solution.py:220
  48.8 6.5 %to_columns.1 = bf16[40,128,128]{2,1,0:T(8,128)(2,1)} custom-call(s32[1]{0:T(128)} %bitcast.me_ref, s32[1]{0:T(128)S(6)} %copy.25.count_ref, s32[160]{0:T(256)S(1)} %copy-done.8, s32[160]{0:T(256)S(1)} %copy-done.9, bf16[160,128,128]{2,1,0:T(8,128)(2,1)S(1)} %get-tuple-element.16.half_ref, bf16[40,128,128]{2,1,0:T(8,128)(2,1)S(1)} %bitcast.11, ...), custom_call_target="tpu_custom_call" | custom-call | tf_op jit(solution)/shard_map/to_columns/pallas_call | solution.py:340
  (35 shorter events, 0.2 us)
Async XLA Ops:
  1.3 20.4 %copy-start.3 = (bf16[128,128]{1,0:T(8,128)(2,1)S(1)}, bf16[128,128]{1,0:T(8,128)(2,1)}, u32[]{:S(2)}) copy-start(bf16[128,128]{1,0:T(8,128)(2,1)} %feat.3) | copy-start | bytes 98308
  1.3 28.4 %copy-start.4 = (bf16[256,256]{1,0:T(8,128)(2,1)S(1)}, bf16[256,256]{1,0:T(8,128)(2,1)}, u32[]{:S(2)}) copy-start(bf16[256,256]{1,0:T(8,128)(2,1)} %w_first.2) | copy-start | bytes 393220
  1.3 28.4 %copy-start.5 = (bf16[256,256]{1,0:T(8,128)(2,1)S(1)}, bf16[256,256]{1,0:T(8,128)(2,1)}, u32[]{:S(2)}) copy-start(bf16[256,256]{1,0:T(8,128)(2,1)} %w_second.2) | copy-start | bytes 393220
  1.3 28.4 %copy-start.7 = (bf16[256,128]{1,0:T(8,128)(2,1)S(1)}, bf16[256,128]{1,0:T(8,128)(2,1)}, u32[]{:S(2)}) copy-start(bf16[256,128]{1,0:T(8,128)(2,1)} %w_third.2) | copy-start | bytes 196612
  1.3 28.4 %copy-start.10 = (f32[256]{0:T(256)S(1)}, f32[256]{0:T(256)}, u32[]{:S(2)}) copy-start(f32[256]{0:T(256)} %param.25) | copy-start | bytes 3076
  1.3 28.4 %copy-start.14 = (f32[128]{0:T(128)S(1)}, f32[128]{0:T(128)}, u32[]{:S(2)}) copy-start(f32[128]{0:T(128)} %param.28) | copy-start | bytes 1540
  1.3 28.4 %copy-start.15 = (f32[128]{0:T(128)S(1)}, f32[128]{0:T(128)}, u32[]{:S(2)}) copy-start(f32[128]{0:T(128)} %param.29) | copy-start | bytes 1540
  6.5 42.2 %copy-start = (bf16[5120,128]{1,0:T(8,128)(2,1)S(1)}, bf16[5120,128]{1,0:T(8,128)(2,1)}, u32[]{:S(2)}) copy-start(bf16[5120,128]{1,0:T(8,128)(2,1)} %param.18) | copy-start | bytes 3932164
  6.5 42.2 %copy-start.1 = (bf16[256,256]{1,0:T(8,128)(2,1)S(1)}, bf16[256,256]{1,0:T(8,128)(2,1)}, u32[]{:S(2)}) copy-start(bf16[256,256]{1,0:T(8,128)(2,1)} %w_first.3) | copy-start | bytes 393220
  6.5 42.2 %copy-start.2 = (bf16[256,256]{1,0:T(8,128)(2,1)S(1)}, bf16[256,256]{1,0:T(8,128)(2,1)}, u32[]{:S(2)}) copy-start(bf16[256,256]{1,0:T(8,128)(2,1)} %w_second.3) | copy-start | bytes 393220
  6.5 42.2 %copy-start.6 = (bf16[256,128]{1,0:T(8,128)(2,1)S(1)}, bf16[256,128]{1,0:T(8,128)(2,1)}, u32[]{:S(2)}) copy-start(bf16[256,128]{1,0:T(8,128)(2,1)} %w_third.3) | copy-start | bytes 196612
  6.5 42.2 %copy-start.8 = (s32[160]{0:T(256)S(1)}, s32[160]{0:T(256)}, u32[]{:S(2)}) copy-start(s32[160]{0:T(256)} %col_ref.1) | copy-start | bytes 1924
  6.6 42.2 %copy-start.9 = (s32[160]{0:T(256)S(1)}, s32[160]{0:T(256)}, u32[]{:S(2)}) copy-start(s32[160]{0:T(256)} %row_ref.1) | copy-start | bytes 1924
  6.6 42.2 %copy-start.11 = (f32[256]{0:T(256)S(1)}, f32[256]{0:T(256)}, u32[]{:S(2)}) copy-start(f32[256]{0:T(256)} %param.31) | copy-start | bytes 3076
  6.6 42.2 %copy-start.12 = (f32[128]{0:T(128)S(1)}, f32[128]{0:T(128)}, u32[]{:S(2)}) copy-start(f32[128]{0:T(128)} %param.34) | copy-start | bytes 1540
  6.6 42.2 %copy-start.13 = (f32[128]{0:T(128)S(1)}, f32[128]{0:T(128)}, u32[]{:S(2)}) copy-start(f32[128]{0:T(128)} %param.35) | copy-start | bytes 1540
  6.6 2.0 %collective-permute-start = (bf16[16,128,128]{2,1,0:T(8,128)(2,1)S(1)}, bf16[16,128,128]{2,1,0:T(8,128)(2,1)S(1)}, u32[]{:S(2)}, u32[]{:S(2)}) collective-permute-start(bf16[16,128,128]{2,1,0:T(8,128)(2,1)S(1)} %get-tuple-element.11), channel_id=1, source_target_pairs={{0,1},{1,0},{2,3},{3,2},{4,5},{5,4},{6,7},{7,6},{8,9},{9,8},{10,11... | collective-permute-start | bytes 1572872 | tf_op jit(solution)/shard_map/ppermute | solution.py:220
  21.7 7.1 %collective-permute-start.1 = (bf16[2,128,128]{2,1,0:T(8,128)(2,1)S(1)}, bf16[2,128,128]{2,1,0:T(8,128)(2,1)S(1)}, u32[]{:S(2)}, u32[]{:S(2)}) collective-permute-start(bf16[2,128,128]{2,1,0:T(8,128)(2,1)S(1)} %get-tuple-element.13), channel_id=1, source_target_pairs={{16,40},{17,41},{18,42},{19,43},{20,44},{21,45},{22,46},{23,47},{2... | collective-permute-start | bytes 196616 | tf_op jit(solution)/shard_map/ppermute | solution.py:220
  25.3 4.4 %collective-permute-start.2 = (bf16[2,128,128]{2,1,0:T(8,128)(2,1)S(1)}, bf16[2,128,128]{2,1,0:T(8,128)(2,1)S(1)}, u32[]{:S(2)}, u32[]{:S(2)}) collective-permute-start(bf16[2,128,128]{2,1,0:T(8,128)(2,1)S(1)} %get-tuple-element.14), channel_id=1, source_target_pairs={{0,24},{1,25},{2,26},{3,27},{4,28},{5,29},{6,30},{7,31},{8,16},{9,... | collective-permute-start | bytes 196616 | tf_op jit(solution)/shard_map/ppermute | solution.py:220
  31.0 3.1 %collective-permute-start.3 = (bf16[2,128,128]{2,1,0:T(8,128)(2,1)S(1)}, bf16[2,128,128]{2,1,0:T(8,128)(2,1)S(1)}, u32[]{:S(2)}, u32[]{:S(2)}) collective-permute-start(bf16[2,128,128]{2,1,0:T(8,128)(2,1)S(1)} %get-tuple-element.17), channel_id=1, source_target_pairs={{0,8},{1,9},{2,10},{3,11},{4,12},{5,13},{6,14},{7,15},{8,0},{9,1},... | collective-permute-start | bytes 196616 | tf_op jit(solution)/shard_map/ppermute | solution.py:220
  34.2 5.4 %collective-permute-start.4 = (bf16[4,128,128]{2,1,0:T(8,128)(2,1)S(1)}, bf16[4,128,128]{2,1,0:T(8,128)(2,1)S(1)}, u32[]{:S(2)}, u32[]{:S(2)}) collective-permute-start(bf16[4,128,128]{2,1,0:T(8,128)(2,1)S(1)} %get-tuple-element.18), channel_id=1, source_target_pairs={{0,2},{1,3},{2,4},{3,5},{4,6},{5,7},{6,0},{7,1},{8,10},{9,11},{10,... | collective-permute-start | bytes 393224 | tf_op jit(solution)/shard_map/ppermute | solution.py:220
  36.6 5.5 %collective-permute-start.5 = (bf16[4,128,128]{2,1,0:T(8,128)(2,1)S(1)}, bf16[4,128,128]{2,1,0:T(8,128)(2,1)S(1)}, u32[]{:S(2)}, u32[]{:S(2)}) collective-permute-start(bf16[4,128,128]{2,1,0:T(8,128)(2,1)S(1)} %get-tuple-element.18), channel_id=1, source_target_pairs={{0,4},{1,5},{2,6},{3,7},{4,0},{5,1},{6,2},{7,3},{8,12},{9,13},{10,... | collective-permute-start | bytes 393224 | tf_op jit(solution)/shard_map/ppermute | solution.py:220
  38.4 3.8 %collective-permute-start.6 = (bf16[4,128,128]{2,1,0:T(8,128)(2,1)S(1)}, bf16[4,128,128]{2,1,0:T(8,128)(2,1)S(1)}, u32[]{:S(2)}, u32[]{:S(2)}) collective-permute-start(bf16[4,128,128]{2,1,0:T(8,128)(2,1)S(1)} %get-tuple-element.18), channel_id=1, source_target_pairs={{0,6},{1,7},{2,0},{3,1},{4,2},{5,3},{6,4},{7,5},{8,14},{9,15},{10,... | collective-permute-start | bytes 393224 | tf_op jit(solution)/shard_map/ppermute | solution.py:220
  42.3 6.5 %collective-permute-start.7 = (bf16[16,128,128]{2,1,0:T(8,128)(2,1)S(1)}, bf16[16,128,128]{2,1,0:T(8,128)(2,1)S(1)}, u32[]{:S(2)}, u32[]{:S(2)}) collective-permute-start(bf16[16,128,128]{2,1,0:T(8,128)(2,1)S(1)} %constant_dynamic-update-slice_fusion.2.near_ref), channel_id=1, source_target_pairs={{0,1},{1,0},{2,3},{3,2},{4,5},{5,4},{6,7},{7,6},{8,9},{9,8},{10,11... | collective-permute-start | bytes 1572872 | tf_op jit(solution)/shard_map/ppermute | solution.py:220
